TPU v7x, 256 devices: a whole 4x4x8 slice. The times are simulated.
256 devices in a mesh: pole: 8 (over z), row: 4 (over x_hi, core), col: 8 (over y, x_lo).
Axes of the slice: x: 4 (x_hi: 2, x_lo: 2; x = x_hi * 2 + x_lo), y: 4, z: 8, core: 2. Of those that a mesh axis runs over, the one named last changes fastest.
Arguments:
- ainv: float32 [8, 8192, 8192], P('pole', 'row', 'col'), may hold values from -6 to 6
- lfac: float32 [8, 8192, 384], P('pole', ('row', 'col')), may hold values from -0.0625 to 0.0625
- dinv: float32 [8, 384, 384], P('pole'), may hold values from -6 to 6
- weights: float32 [8], P('pole'), may hold values from 0.1 to 1
- present: int32 [32], replicated, may hold values 0 or 1
Outputs:
- ainv_col: float32 [8, 8192, 384], P('pole', ('row', 'col'))
- ainv_diag: float32 [8, 384, 384], P('pole')
- dm_col: float32 [8192, 384], P(('row', 'col'))
- dm_diag: float32 [384, 384], replicated
All inputs are finite; a program needn't handle non-finite values.
Results may differ from a plain program's by a relative error of at most 0.000071.
Values sent between devices are 32-bit elements; how exact they have to be, the bound alone decides.
No kernel may reach another device: no remote copies, remote signals or barrier semaphores. Data moves between devices by JAX's collectives and lax.ppermute only.
A program may use at most 128 MiB of HBM per device.

v0:
```python
import jax
import jax.numpy as jnp
from jax import lax
from jax.sharding import PartitionSpec as P


def on_device(ainv, lfac, dinv, weights, present):
    row_size = lax.axis_size("row")
    col_size = lax.axis_size("col")
    rows_dev = lfac.shape[1]
    row_index = lax.axis_index("row")
    col_index = lax.axis_index("col")
    block_index = row_index * col_size + col_index
    present_own = lax.dynamic_index_in_dim(present, block_index, 0, keepdims=False).astype(
        jnp.float32
    )
    masked = lfac[0] * present_own
    col_rows = row_size * rows_dev
    gathered = lax.all_gather(masked, ("row", "col"), axis=0, tiled=True)
    panel = lax.dynamic_slice_in_dim(gathered, col_index * col_rows, col_rows, 0)
    inverse = ainv[0]
    column_block = -(
        present_own
        * lax.psum_scatter(
            jnp.dot(
                inverse, panel, precision=lax.Precision.HIGHEST, preferred_element_type=jnp.float32
            ),
            "col",
            scatter_dimension=0,
            tiled=True,
        )
    )
    correction = lax.psum(
        jnp.dot(
            masked.T,
            column_block,
            precision=lax.Precision.HIGHEST,
            preferred_element_type=jnp.float32,
        ),
        ("row", "col"),
    )
    diagonal = dinv[0] - correction
    weight_here = weights[0]
    dm_col, dm_diag = lax.psum((weight_here * column_block, weight_here * diagonal), "pole")
    return (column_block[None], diagonal[None], dm_col, dm_diag)


def solution(mesh):
    return jax.shard_map(
        on_device,
        mesh=mesh,
        in_specs=(
            P("pole", "row", "col"),
            P("pole", ("row", "col"), None),
            P("pole", None, None),
            P("pole"),
            P(),
        ),
        out_specs=(
            P("pole", ("row", "col"), None),
            P("pole", None, None),
            P(("row", "col"), None),
            P(),
        ),
        check_vma=False,
    )
```

profile of v0, /device:TPU:8, one launch (start us, length us, event | category | flops | bytes accessed | tf_op | source)
XLA Modules:
  0.0 418.8 jit_solution(1551533651714790682)
XLA Ops:
  7.2 0.0 all-gather.3.cloned.1.call-start
  7.2 1.2 dynamic_slice.7
  9.1 1.8 broadcast_multiply_fusion.1
  10.9 0.0 copy-start
  10.9 0.0 all-gather.3.cloned.1.call-update
  10.9 0.0 reduce-scatter.2.cloned.1.call-start
  11.0 0.0 copy-start.1
  11.0 103.2 %all-gather.3.cloned.1.call-done = f32[1,8192,384]{2,1,0:T(8,128)} async-done(((f32[1,256,384]{2,1,0:T(8,128)}), f32[1,8192,384]{2,1,0:T(8,128)}) %all-gather.3.cloned.1.call-update) | async-done | bytes 12582928 | tf_op jit(solution)/shard_map/all_gather | solution.py:19
  114.2 23.7 %fusion.2 = f32[2048,384]{0,1:T(8,128)} fusion(f32[1,2048,1024]{2,1,0:T(8,128)} %param.5, f32[1,8192,384]{2,1,0:T(8,128)} %all-gather.3.cloned.1.call-done, s32[]{:T(128)S(6)} %select_n.8), kind=kOutput, calls=%fused_computation.2 | convolution fusion | flops 9663676416 | bytes 13107204 | tf_op jit(solution)/shard_map/dot_general | solution.py:25
  137.9 0.0 reduce-scatter.2.cloned.1.call-update
  138.0 0.0 all-reduce.4.cloned.1.call-start
  138.0 74.5 %reduce-scatter.2.cloned.1.call-done = f32[256,384]{0,1:T(8,128)} async-done(((f32[2048,384]{0,1:T(8,128)}), f32[256,384]{0,1:T(8,128)}) %reduce-scatter.2.cloned.1.call-update) | async-done | bytes 393232 | tf_op jit(solution)/shard_map/reduce_scatter | solution.py:24
  212.5 0.0 copy-done
  212.5 3.2 fusion.7
  215.8 0.0 all-reduce.4.cloned.1.call-update
  215.8 0.0 all-reduce.6.cloned.1.call-start
  216.5 1.8 fusion.9
  218.3 111.5 %all-reduce.4.cloned.1.call-done = f32[384,384]{1,0:T(8,128)} async-done(((f32[384,384]{1,0:T(8,128)}), f32[384,384]{1,0:T(8,128)}) %all-reduce.4.cloned.1.call-update) | async-done | bytes 589840 | tf_op jit(solution)/shard_map/psum | solution.py:33
  329.8 0.0 copy-done.1
  329.8 2.2 broadcast_multiply_fusion
  331.9 0.0 all-reduce.6.cloned.1.call-update
  332.0 0.9 copy.9
  332.9 75.5 %all-reduce.6.cloned.1.call-done = (f32[256,384]{0,1:T(8,128)}, f32[384,384]{1,0:T(8,128)}) async-done(((f32[256,384]{0,1:T(8,128)}, f32[384,384]{1,0:T(8,128)}), (f32[256,384]{0,1:T(8,128)}, f32[384,384]{1,0:T(8,128)})) %all-reduce.6.cloned.1.call-update) | async-done | bytes 983056 | tf_op jit(solution)/shard_map/psum | solution.py:44
  408.4 1.9 copy.10
  410.3 1.9 copy.15
Async XLA Ops:
  7.2 107.1 %all-gather.3.cloned.1.call-start = ((), (), s32[]{:S(2)}) async-start(), calls=%async_computation.3 | async-start | bytes 12976128 | tf_op jit(solution)/shard_map/all_gather | solution.py:19
  10.9 201.7 %copy-start = (f32[1,256,384]{2,1,0:T(8,128)S(1)}, f32[1,256,384]{2,1,0:T(8,128)}, u32[]{:S(2)}) copy-start(f32[1,256,384]{2,1,0:T(8,128)} %param.6) | copy-start | bytes 1179652
  10.9 201.6 %reduce-scatter.2.cloned.1.call-start = ((), (), s32[]{:S(2)}) async-start(), calls=%async_computation.1 | async-start | bytes 3538944 | tf_op jit(solution)/shard_map/reduce_scatter | solution.py:24
  11.0 318.8 %copy-start.1 = (f32[1,384,384]{2,1,0:T(8,128)S(1)}, f32[1,384,384]{2,1,0:T(8,128)}, u32[]{:S(2)}) copy-start(f32[1,384,384]{2,1,0:T(8,128)} %param.7) | copy-start | bytes 1769476
  138.0 191.8 %all-reduce.4.cloned.1.call-start = ((), (), s32[]{:S(2)}) async-start(), calls=%async_computation.2 | async-start | bytes 1179648 | tf_op jit(solution)/shard_map/psum | solution.py:33
  215.8 192.6 %all-reduce.6.cloned.1.call-start = ((), (), s32[]{:S(2)}) async-start(), calls=%async_computation.4 | async-start | bytes 1966080 | tf_op jit(solution)/shard_map/psum | solution.py:44
Sparse Core Ops, SparseCore 0:
  11.0 103.1 all-gather.2
  138.1 74.4 reduce-scatter.1
  216.4 113.3 all-reduce.3
  332.6 75.7 all-reduce.5
where the time goes:
time: 419 us
  waiting for transfers between devices  365 us (87%)
  matrix products  27 us (6%)
  between operations  15.1 us (4%)
  local copies, waits for them, and re-layouts  5.99 us (1%)
  other arithmetic  5.73 us (1%)
    psum x1, waiting for transfers between devices, on_device(): lax.psum(jnp.dot(masked.T, column_block, precision=lax.Precision.HIGHEST,...  111 us
    all_gather x1, waiting for transfers between devices, on_device(): gathered = lax.all_gather(masked, ('row', 'col'), axis=0, tiled=True)  103 us
    psum x1, waiting for transfers between devices, on_device(): lax.psum((weight_here * column_block, weight_here * diagonal), 'pole')  75.5 us
    reduce_scatter x1, waiting for transfers between devices, on_device(): lax.psum_scatter(jnp.dot(inverse, panel, precision=lax.Precision.HIGHEST,...  74.5 us
    dot_general x1, matrix products, on_device(): jnp.dot(inverse, panel, precision=lax.Precision.HIGHEST, preferred_elemen...  23.7 us
  transfers between devices with their start and end apart: 4, of which 4 were waited for; matrix products, arithmetic and copies ran while one was open for 1% of the time, Pallas kernels for 0%

commit v1 on v0

v1 whole, which is shorter than its diff:
```python
import jax
import jax.numpy as jnp
from jax import lax
from jax.experimental import pallas as pl
from jax.experimental.pallas import tpu as pltpu
from jax.sharding import PartitionSpec as P

PLANE = ("row", "col")
MIB = 1 << 20


def place(x, y, core):
    return ((x // 2) * 2 + core) * 8 + y * 2 + x % 2


CHIPS = [(x, y, core) for x in range(4) for y in range(4) for core in range(2)]


def shift(value, dx=0, dy=0, other=0):
    pairs = [(place(x, y, c), place((x + dx) % 4, (y + dy) % 4, c ^ other)) for x, y, c in CHIPS]
    return lax.ppermute(value, PLANE, pairs)


def flip_x(value):
    return lax.ppermute(value, PLANE, [(place(x, y, c), place(x ^ 1, y, c)) for x, y, c in CHIPS])


def along_pole(value, step):
    return lax.ppermute(value, "pole", [(z, (z + step) % 8) for z in range(8)])


def pole_pair(value):
    return lax.ppermute(value, "pole", [(z, z ^ 1) for z in range(8)])


def panel_slot(value, j):
    pairs = []
    for x, y, c in CHIPS:
        k = 2 * c + (j ^ (x // 2))
        source = place((y // 2) * 2 + k % 2, 2 * (x % 2) + k // 2, y % 2)
        pairs.append((source, place(x, y, c)))
    return lax.ppermute(value, PLANE, pairs)


def split(value):
    high = value.astype(jnp.bfloat16)
    return high, (value - high.astype(jnp.float32)).astype(jnp.bfloat16)


def mm(a, b, contract=((1,), (0,))):
    return lax.dot_general(a, b, (contract, ((), ())), preferred_element_type=jnp.float32)


def mm3(a_high, a_low, b_high, b_low, contract=((1,), (0,))):
    return mm(a_high, b_high, contract) + (mm(a_high, b_low, contract) + mm(a_low, b_high, contract))


def first_kernel(info, inverse, s0, s1, t0, t1, out, high, low):
    rows = s0.shape[0]

    @pl.when(pl.program_id(0) == 0)
    def _():
        for i, slot in enumerate((s0, s1, t0, t1)):
            at = pl.ds(pl.multiple_of(info[1 + i] * rows, rows), rows)
            keep = (info[5 + i] > 0).astype(jnp.float32)
            high[at, :], low[at, :] = split(slot[...] * keep)

    out[...] = mm3(*split(inverse[...]), high[...], low[...])


def next_kernel(info, inverse, high, low, out):
    out[...] = mm3(*split(inverse[...]), high[...], low[...])


def chunk_dot(info, inverse, panel, rows, tile=256):
    depth = inverse.shape[1]
    width = panel[0].shape[1]
    first = len(panel) == 4
    steps = 2 * rows // tile
    whole = pl.BlockSpec(memory_space=pltpu.VMEM)
    out_shape = [jax.ShapeDtypeStruct((2 * rows, width), jnp.float32)]
    out_specs = [pl.BlockSpec((tile, width), lambda i, info: (i, 0))]
    if first:
        out_shape += [jax.ShapeDtypeStruct((depth, width), jnp.bfloat16)] * 2
        out_specs += [whole] * 2
    return pl.pallas_call(
        first_kernel if first else next_kernel,
        out_shape=out_shape,
        grid_spec=pltpu.PrefetchScalarGridSpec(
            num_scalar_prefetch=1,
            grid=(steps,),
            in_specs=[pl.BlockSpec((tile, depth), lambda i, info: (info[0] * steps + i, 0))]
            + [whole] * len(panel),
            out_specs=out_specs,
        ),
        cost_estimate=pl.CostEstimate(
            flops=6 * 2 * rows * depth * width,
            bytes_accessed=4 * (2 * rows * depth + 2 * rows * width + depth * width),
            transcendentals=0,
        ),
        compiler_params=pltpu.CompilerParams(vmem_limit_bytes=32 * MIB),
    )(info, inverse, *panel)


def corr_kernel(info, p0, u_first, u_second, d_first, d_second, own, other, corr, s_own, s_other):
    rows = own.shape[0]
    at_own, at_other = info[0], info[1]
    first = p0[:rows] + (u_first[...] + d_first[...])
    second = p0[rows:] + (u_second[...] + d_second[...])
    own_is_first = at_own == 0
    sum_own = jnp.where(own_is_first, first, second)
    sum_other = jnp.where(own_is_first, second, first)
    keep_own = (info[2] > 0).astype(jnp.float32)
    keep_other = (info[3] > 0).astype(jnp.float32)
    sum_own = sum_own * keep_own
    sum_other = sum_other * keep_other
    s_own[...] = sum_own
    s_other[...] = sum_other
    by_rows = ((0,), (0,))
    corr[...] = mm3(*split(own[...]), *split(sum_own), by_rows) + mm3(
        *split(other[...]), *split(sum_other), by_rows
    )


def correction(info, *arrays):
    rows, width = arrays[-1].shape
    vmem = pl.BlockSpec(memory_space=pltpu.VMEM)
    return pl.pallas_call(
        corr_kernel,
        out_shape=[
            jax.ShapeDtypeStruct((width, width), jnp.float32),
            jax.ShapeDtypeStruct((rows, width), jnp.float32),
            jax.ShapeDtypeStruct((rows, width), jnp.float32),
        ],
        in_specs=[pl.BlockSpec(memory_space=pltpu.SMEM)] + [vmem] * len(arrays),
        out_specs=[vmem] * 3,
        cost_estimate=pl.CostEstimate(
            flops=12 * rows * width * width, bytes_accessed=36 * rows * width, transcendentals=0
        ),
        compiler_params=pltpu.CompilerParams(vmem_limit_bytes=32 * MIB),
    )(info, *arrays)


def part(value, index, size):
    return lax.dynamic_slice_in_dim(value, index * size, size, 0)


def ring_scatter(value, me, size, send):
    away = [send(part(value, (me + k) % 4, size), k) for k in (1, 2, 3)]
    return (part(value, me, size) + away[1]) + (away[0] + away[2])


def ring_gather(value, me, send):
    size = value.shape[0]
    rising = [send(value, 3), send(value, 2), send(value, 1), value]
    twice = jnp.concatenate(rising + rising[:3], 0)
    return lax.dynamic_slice_in_dim(twice, (3 - me) * size, 4 * size, 0)


def pair_gather(value, me, swap):
    other = swap(value)
    size = value.shape[0]
    thrice = jnp.concatenate([other, value, other], 0)
    return lax.dynamic_slice_in_dim(thrice, (1 - me) * size, 2 * size, 0)


def on_device(ainv, lfac, dinv, weights, present):
    own = lfac[0]
    rows, width = own.shape
    row, col = lax.axis_index("row"), lax.axis_index("col")
    z = lax.axis_index("pole")
    x_hi, core = row // 2, row % 2
    y, x_lo = col // 2, col % 2
    x = x_hi * 2 + x_lo
    half, quarter = width // 2, width // 8

    def sibling(v):
        return shift(v, other=1)

    slots = [panel_slot(own, 0), panel_slot(own, 1)]
    slots += [sibling(s) for s in slots]
    other = flip_x(own)
    order = jnp.stack([2 * core + x_hi, 2 * core + 1 - x_hi, 2 * (1 - core) + x_hi, 2 * (1 - core) + 1 - x_hi])
    kept = jnp.take(present, 4 * col + order)

    def info(d):
        return jnp.concatenate([((y + d) % 4)[None], order, kept]).astype(jnp.int32)

    inverse = ainv[0]
    p2, high, low = chunk_dot(info(2), inverse, slots, rows)
    r_up = shift(p2[:rows], dy=1)
    r_down = shift(p2[rows:], dy=-1)
    (p1,) = chunk_dot(info(1), inverse, (high, low), rows)
    u_second = shift(p1[rows:], dy=1)
    (p3,) = chunk_dot(info(3), inverse, (high, low), rows)
    d_first = shift(p3[:rows], dy=-1)
    (p0,) = chunk_dot(info(0), inverse, (high, low), rows)
    u_first = shift(p1[:rows] + r_up, dy=1)
    d_second = shift(p3[rows:] + r_down, dy=-1)

    keep = jnp.take(present, row * 8 + jnp.stack([col, col ^ 1]))
    tail = jnp.concatenate([jnp.stack([x_lo, 1 - x_lo]), keep]).astype(jnp.int32)
    corr, s_own, s_other = correction(tail, p0, u_first, u_second, d_first, d_second, own, other)

    column = -(s_own + flip_x(s_other))

    mine = part(corr, core, half) + sibling(part(corr, 1 - core, half))
    mine = ring_scatter(mine, x, quarter, lambda v, k: shift(v, dx=k))
    mine = (mine + shift(mine, dy=2)) + (shift(mine, dy=1) + shift(mine, dy=3))
    diagonal = lax.dynamic_slice_in_dim(dinv[0], core * half + x * quarter, quarter, 0) + mine

    def spread(v):
        v = ring_gather(v, x, lambda u, k: shift(u, dx=k))
        return pair_gather(v, core, sibling)

    weight = weights[0]
    part_dm = weight * diagonal
    part_dm = part_dm + pole_pair(part_dm)
    part_dm = (part_dm + along_pole(part_dm, 4)) + (along_pole(part_dm, 2) + along_pole(part_dm, 6))

    pair, four = z % 2, z // 2
    weighted = weight * column
    dm = part(weighted, pair, rows // 2) + pole_pair(part(weighted, 1 - pair, rows // 2))
    dm = ring_scatter(dm, four, rows // 8, lambda v, k: along_pole(v, 2 * k))
    dm = ring_gather(dm, four, lambda v, k: along_pole(v, 2 * k))
    dm = pair_gather(dm, pair, pole_pair)

    return column[None], spread(diagonal)[None], dm, spread(part_dm)


def solution(mesh):
    return jax.shard_map(
        on_device,
        mesh=mesh,
        in_specs=(
            P("pole", "row", "col"),
            P("pole", ("row", "col"), None),
            P("pole", None, None),
            P("pole"),
            P(),
        ),
        out_specs=(
            P("pole", ("row", "col"), None),
            P("pole", None, None),
            P(("row", "col"), None),
            P(),
        ),
        check_vma=False,
    )
```

time: 419 us -> 146 us (0.35)
  waiting for transfers between devices: 365 us -> 47.1 us
  starting transfers between devices: 0.16 us -> 68.3 us
  matrix products: 27 us -> 0 us
  between operations: 15.1 us -> 1.81 us
  Pallas kernels: 0 us -> 12 us
    psum x2 -> x0, waiting for transfers between devices: 187 us -> none  [the longest x1 111 us: on_device(): lax.psum(jnp.dot(masked.T, column_block, precision=lax.Precision.HIGHEST,...]
    all_gather x1 -> x0, waiting for transfers between devices: 103 us -> none  [on_device(): gathered = lax.all_gather(masked, ('row', 'col'), axis=0, tiled=True)]
    reduce_scatter x1 -> x0, waiting for transfers between devices: 74.5 us -> none  [on_device(): lax.psum_scatter(jnp.dot(inverse, panel, precision=lax.Precision.HIGHEST,...]
    ppermute x0 -> x39, starting transfers between devices: none -> 68.3 us  [the longest x23 26.4 us: shift(): return lax.ppermute(value, PLANE, pairs)]
    ppermute x0 -> x39, waiting for transfers between devices: none -> 47.1 us  [the longest x23 27.1 us: shift(): return lax.ppermute(value, PLANE, pairs)]
    dot_general x2 -> x0, matrix products: 27 us -> none  [the longest x1 23.7 us: on_device(): jnp.dot(inverse, panel, precision=lax.Precision.HIGHEST, preferred_elemen...]
    pallas_call x0 -> x5, Pallas kernels: none -> 12 us  [the longest x4 10.5 us: chunk_dot(): pl.pallas_call(first_kernel if first else next_kernel, out_shape=out_shap...]
  transfers between devices with their start and end apart: 4 -> 39, of which waited for: 4 -> 15; matrix products, arithmetic and copies ran while one was open for 1% -> 4% of each run, Pallas kernels for 0% -> 5%
where the time goes in v1:
time: 146 us; the launch traced here: 144 us
  starting transfers between devices  68.3 us (47%)
  waiting for transfers between devices  47.1 us (32%)
  Pallas kernels  12 us (8%)
  local copies, waits for them, and re-layouts  8.75 us (6%)
  other arithmetic  6.44 us (4%)
  between operations  1.81 us (1%)
    ppermute x23, waiting for transfers between devices, shift(): return lax.ppermute(value, PLANE, pairs)  27.1 us
    ppermute x23, starting transfers between devices, shift(): return lax.ppermute(value, PLANE, pairs)  26.4 us
    ppermute x9, starting transfers between devices, along_pole(): return lax.ppermute(value, 'pole', [(z, (z + step) % 8) for z in range(8)])  21.6 us
    pallas_call x4, Pallas kernels, chunk_dot(): pl.pallas_call(first_kernel if first else next_kernel, out_shape=out_shap...  10.5 us
    ppermute x2, waiting for transfers between devices, panel_slot(): return lax.ppermute(value, PLANE, pairs)  10.3 us
    ppermute x2, starting transfers between devices, flip_x(): lax.ppermute(value, PLANE, [(place(x, y, c), place(x ^ 1, y, c)) for x, y...  9.5 us
    ppermute x2, starting transfers between devices, panel_slot(): return lax.ppermute(value, PLANE, pairs)  7.7 us
    unnamed x26, local copies, waits for them, and re-layouts  6.89 us
  transfers between devices with their start and end apart: 39, of which 15 were waited for; matrix products, arithmetic and copies ran while one was open for 4% of the time, Pallas kernels for 5%

profile of v1, /device:TPU:8, one launch (start us, length us, event | category | flops | bytes accessed | tf_op | source)
XLA Modules:
  0.0 144.4 jit_solution(8886147781600163285)
XLA Ops:
  0.7 2.1 %collective-permute-start = (f32[256,384]{1,0:T(8,128)}, f32[256,384]{1,0:T(8,128)S(1)}, u32[]{:S(2)}, u32[]{:S(2)}) collective-permute-start(f32[256,384]{1,0:T(8,128)} %bitcast.38), channel_id=1, source_target_pairs={{0,0},{2,8},{8,2},{10,10},{16,4},{18,12},{24,6},{26,14},{4,1},{6,9... | collective-permute-start | bytes 1179656 | tf_op jit(solution)/shard_map/ppermute | solution.py:42
  2.7 5.7 %collective-permute-start.1 = (f32[256,384]{1,0:T(8,128)}, f32[256,384]{1,0:T(8,128)S(1)}, u32[]{:S(2)}, u32[]{:S(2)}) collective-permute-start(f32[256,384]{1,0:T(8,128)} %bitcast.39), channel_id=1, source_target_pairs={{1,0},{3,8},{9,2},{11,10},{17,4},{19,12},{25,6},{27,14},{5,1},{7,9... | collective-permute-start | bytes 1179656 | tf_op jit(solution)/shard_map/ppermute | solution.py:42
  8.4 10.3 %collective-permute-done.s0 = f32[256,384]{1,0:T(8,128)S(1)} collective-permute-done((f32[256,384]{1,0:T(8,128)}, f32[256,384]{1,0:T(8,128)S(1)}, u32[]{:S(2)}, u32[]{:S(2)}) %collective-permute-start) | collective-permute-done | bytes 393248 | tf_op jit(solution)/shard_map/ppermute | solution.py:42
  21.1 3.4 %copy-done.1 = f32[1,2048,1024]{2,1,0:T(8,128)S(1)} copy-done((f32[1,2048,1024]{2,1,0:T(8,128)S(1)}, f32[1,2048,1024]{2,1,0:T(8,128)}, u32[]{:S(2)}) %copy-start.1) | copy-done | bytes 8388632
  24.5 2.9 %shard_map.84 = (f32[512,384]{1,0:T(8,128)S(1)}, bf16[1024,384]{1,0:T(8,128)(2,1)S(1)}, bf16[1024,384]{1,0:T(8,128)(2,1)S(1)}) custom-call(s32[9]{0:T(128)S(1)} %concatenate.57.info, f32[2048,1024]{1,0:T(8,128)S(1)} %bitcast.34, f32[256,384]{1,0:T(8,128)S(1)} %collective-permute-done.s0, f32[256,384]{1,0:T(8,128)S(1)} %collective-permute-done.1.s1, ...), custom_call_target="tpu_custom_call" | custom-call | flops 1207959552 | bytes 4456448 | tf_op jit(solution)/shard_map/pallas_call | solution.py:86
  28.0 7.7 %collective-permute-start.10 = (f32[256,384]{1,0:T(8,128)S(1)}, f32[256,384]{1,0:T(8,128)S(1)}, u32[]{:S(2)}, u32[]{:S(2)}) collective-permute-start(f32[256,384]{1,0:T(8,128)S(1)} %bitcast.40), channel_id=1, source_target_pairs={{0,1},{8,9},{2,3},{10,11},{4,5},{12,13},{6,7},{14,15},{1,0},{9,8},... | collective-permute-start | bytes 1179656 | tf_op jit(solution)/shard_map/ppermute | solution.py:25
  37.2 3.4 %copy-done.2 = f32[1,2048,1024]{2,1,0:T(8,128)S(1)} copy-done((f32[1,2048,1024]{2,1,0:T(8,128)S(1)}, f32[1,2048,1024]{2,1,0:T(8,128)}, u32[]{:S(2)}) %copy-start.2) | copy-done | bytes 8388632
  40.6 2.6 %shard_map.87 = f32[512,384]{1,0:T(8,128)S(1)} custom-call(s32[9]{0:T(128)S(1)} %concatenate.59.info, f32[2048,1024]{1,0:T(8,128)S(1)} %bitcast.35, bf16[1024,384]{1,0:T(8,128)(2,1)S(1)} %get-tuple-element.10.high, bf16[1024,384]{1,0:T(8,128)(2,1)S(1)} %get-tuple-element.11.low), custom_call_target="tpu_custom_call" | custom-call | flops 1207959552 | bytes 4456448 | tf_op jit(solution)/shard_map/pallas_call | solution.py:86
  43.2 2.6 %shard_map.86 = f32[512,384]{1,0:T(8,128)S(1)} custom-call(s32[9]{0:T(128)S(1)} %concatenate.58.info, f32[2048,1024]{1,0:T(8,128)S(1)} %bitcast.36, bf16[1024,384]{1,0:T(8,128)(2,1)S(1)} %get-tuple-element.10.high, bf16[1024,384]{1,0:T(8,128)(2,1)S(1)} %get-tuple-element.11.low), custom_call_target="tpu_custom_call" | custom-call | flops 1207959552 | bytes 4456448 | tf_op jit(solution)/shard_map/pallas_call | solution.py:86
  45.8 1.1 slice_add_fusion
  46.9 1.6 %collective-permute-start.7 = (f32[256,384]{1,0:T(8,128)S(1)}, f32[256,384]{1,0:T(8,128)S(1)}, u32[]{:S(2)}, u32[]{:S(2)}) collective-permute-start(f32[256,384]{1,0:T(8,128)S(1)} %get-tuple-element.21), channel_id=1, source_target_pairs={{0,6},{8,14},{2,0},{10,8},{4,2},{12,10},{6,4},{14,12},{1,7},{9,15}... | collective-permute-start | bytes 1179656 | tf_op jit(solution)/shard_map/ppermute | solution.py:21
  48.5 3.2 %collective-permute-start.9 = (f32[256,384]{1,0:T(8,128)S(1)}, f32[256,384]{1,0:T(8,128)S(1)}, u32[]{:S(2)}, u32[]{:S(2)}) collective-permute-start(f32[256,384]{1,0:T(8,128)S(1)} %get-tuple-element.20), channel_id=1, source_target_pairs={{0,6},{8,14},{2,0},{10,8},{4,2},{12,10},{6,4},{14,12},{1,7},{9,15}... | collective-permute-start | bytes 1179656 | tf_op jit(solution)/shard_map/ppermute | solution.py:21
  52.3 2.5 %shard_map.85.p0 = f32[512,384]{1,0:T(8,128)S(1)} custom-call(s32[9]{0:T(128)S(1)} %concatenate.56.info, f32[2048,1024]{1,0:T(8,128)S(1)} %bitcast.37, bf16[1024,384]{1,0:T(8,128)(2,1)S(1)} %get-tuple-element.10.high, bf16[1024,384]{1,0:T(8,128)(2,1)S(1)} %get-tuple-element.11.low), custom_call_target="tpu_custom_call" | custom-call | flops 1207959552 | bytes 4456448 | tf_op jit(solution)/shard_map/pallas_call | solution.py:86
  54.8 4.1 %collective-permute-done.7.d_first = f32[256,384]{1,0:T(8,128)S(1)} collective-permute-done((f32[256,384]{1,0:T(8,128)S(1)}, f32[256,384]{1,0:T(8,128)S(1)}, u32[]{:S(2)}, u32[]{:S(2)}) %collective-permute-start.7) | collective-permute-done | bytes 393248 | tf_op jit(solution)/shard_map/ppermute | solution.py:21
  58.9 7.3 %collective-permute-done.9.d_second = f32[256,384]{1,0:T(8,128)S(1)} collective-permute-done((f32[256,384]{1,0:T(8,128)S(1)}, f32[256,384]{1,0:T(8,128)S(1)}, u32[]{:S(2)}, u32[]{:S(2)}) %collective-permute-start.9) | collective-permute-done | bytes 393248 | tf_op jit(solution)/shard_map/ppermute | solution.py:21
  66.2 4.1 %collective-permute-done.6.u_second = f32[256,384]{1,0:T(8,128)S(1)} collective-permute-done((f32[256,384]{1,0:T(8,128)S(1)}, f32[256,384]{1,0:T(8,128)S(1)}, u32[]{:S(2)}, u32[]{:S(2)}) %collective-permute-start.6) | collective-permute-done | bytes 393248 | tf_op jit(solution)/shard_map/ppermute | solution.py:21
  70.3 1.4 %shard_map.88 = (f32[384,384]{1,0:T(8,128)S(1)}, f32[256,384]{1,0:T(8,128)S(1)}, f32[256,384]{1,0:T(8,128)S(1)}) custom-call(s32[4]{0:T(128)S(1)} %pad_add_fusion.info, f32[512,384]{1,0:T(8,128)S(1)} %shard_map.85.p0, f32[256,384]{1,0:T(8,128)S(1)} %collective-permute-done.5.u_first, f32[256,384]{1,0:T(8,128)S(1)} %collective-permute-done.6.u_second, ...), custom_call_target="tpu_custom_call" | custom-call | flops 452984832 | bytes 3538944 | tf_op jit(solution)/shard_map/pallas_call | solution.py:128
  72.0 1.8 %collective-permute-start.11 = (f32[256,384]{1,0:T(8,128)S(1)}, f32[256,384]{1,0:T(8,128)S(1)}, u32[]{:S(2)}, u32[]{:S(2)}) collective-permute-start(f32[256,384]{1,0:T(8,128)S(1)} %get-tuple-element.14), channel_id=1, source_target_pairs={{0,1},{8,9},{2,3},{10,11},{4,5},{12,13},{6,7},{14,15},{1,0},{9,8},... | collective-permute-start | bytes 1179656 | tf_op jit(solution)/shard_map/ppermute | solution.py:25
  73.9 1.6 %collective-permute-start.13 = (f32[48,384]{1,0:T(8,128)S(1)}, f32[48,384]{1,0:T(8,128)S(1)}, u32[]{:S(2)}, u32[]{:S(2)}) collective-permute-start(f32[48,384]{1,0:T(8,128)S(1)} %get-tuple-element.26), channel_id=1, source_target_pairs={{0,16},{8,24},{2,18},{10,26},{4,20},{12,28},{6,22},{14,30},{1,17},... | collective-permute-start | bytes 221192 | tf_op jit(solution)/shard_map/ppermute | solution.py:21
  75.6 3.2 %collective-permute-start.15 = (f32[48,384]{1,0:T(8,128)S(1)}, f32[48,384]{1,0:T(8,128)S(1)}, u32[]{:S(2)}, u32[]{:S(2)}) collective-permute-start(f32[48,384]{1,0:T(8,128)S(1)} %get-tuple-element.27), channel_id=1, source_target_pairs={{0,17},{8,25},{2,19},{10,27},{4,21},{12,29},{6,23},{14,31},{1,0},{... | collective-permute-start | bytes 221192 | tf_op jit(solution)/shard_map/ppermute | solution.py:21
  79.5 6.4 %collective-permute-done.13 = f32[48,384]{1,0:T(8,128)S(1)} collective-permute-done((f32[48,384]{1,0:T(8,128)S(1)}, f32[48,384]{1,0:T(8,128)S(1)}, u32[]{:S(2)}, u32[]{:S(2)}) %collective-permute-start.13) | collective-permute-done | bytes 73760 | tf_op jit(solution)/shard_map/ppermute | solution.py:21
  85.9 0.7 collective-permute-done.15
  87.2 2.6 %collective-permute-start.17 = (f32[48,384]{1,0:T(8,128)S(1)}, f32[48,384]{1,0:T(8,128)S(1)}, u32[]{:S(2)}, u32[]{:S(2)}) collective-permute-start(f32[48,384]{1,0:T(8,128)S(1)} %add_add_fusion.1), channel_id=1, source_target_pairs={{0,2},{8,10},{2,4},{10,12},{4,6},{12,14},{6,0},{14,8},{1,3},{9,11}... | collective-permute-start | bytes 221192 | tf_op jit(solution)/shard_map/ppermute | solution.py:21
  89.8 0.8 broadcast_multiply_fusion
  90.6 2.8 %collective-permute-done.16 = f32[48,384]{1,0:T(8,128)S(1)} collective-permute-done((f32[48,384]{1,0:T(8,128)S(1)}, f32[48,384]{1,0:T(8,128)S(1)}, u32[]{:S(2)}, u32[]{:S(2)}) %collective-permute-start.16) | collective-permute-done | bytes 73760 | tf_op jit(solution)/shard_map/ppermute | solution.py:21
  93.3 0.8 collective-permute-done.18
  94.1 0.9 broadcast_multiply_fusion.1
  95.0 2.0 %collective-permute-start.31 = (f32[48,384]{1,0:T(8,128)S(1)}, f32[48,384]{1,0:T(8,128)S(1)}, u32[]{:S(2)}, u32[]{:S(2)}) collective-permute-start(f32[48,384]{1,0:T(8,128)S(1)} %get-tuple-element.16), channel_id=1, source_target_pairs={{0,32},{32,0},{64,96},{96,64},{128,160},{160,128},{192,224},{224,1... | collective-permute-start | bytes 221192 | tf_op jit(solution)/shard_map/ppermute | solution.py:33
  97.0 1.7 %collective-permute-start.19 = (f32[48,384]{1,0:T(8,128)S(1)}, f32[48,384]{1,0:T(8,128)S(1)}, u32[]{:S(2)}, u32[]{:S(2)}) collective-permute-start(f32[48,384]{1,0:T(8,128)S(1)} %get-tuple-element.17), channel_id=1, source_target_pairs={{0,17},{8,25},{2,19},{10,27},{4,21},{12,29},{6,23},{14,31},{1,0},{... | collective-permute-start | bytes 221192 | tf_op jit(solution)/shard_map/ppermute | solution.py:21
  98.9 2.1 %collective-permute-start.20 = (f32[48,384]{1,0:T(8,128)S(1)}, f32[48,384]{1,0:T(8,128)S(1)}, u32[]{:S(2)}, u32[]{:S(2)}) collective-permute-start(f32[48,384]{1,0:T(8,128)S(1)} %get-tuple-element.17), channel_id=1, source_target_pairs={{0,16},{8,24},{2,18},{10,26},{4,20},{12,28},{6,22},{14,30},{1,17},... | collective-permute-start | bytes 221192 | tf_op jit(solution)/shard_map/ppermute | solution.py:21
  101.1 7.2 %collective-permute-start.32 = (f32[48,384]{1,0:T(8,128)S(1)}, f32[48,384]{1,0:T(8,128)S(1)}, u32[]{:S(2)}, u32[]{:S(2)}) collective-permute-start(f32[48,384]{1,0:T(8,128)S(1)} %add.338), channel_id=1, source_target_pairs={{0,128},{32,160},{64,192},{96,224},{128,0},{160,32},{192,64},{224,... | collective-permute-start | bytes 221192 | tf_op jit(solution)/shard_map/ppermute | solution.py:29
  108.3 1.5 %collective-permute-start.33 = (f32[48,384]{1,0:T(8,128)S(1)}, f32[48,384]{1,0:T(8,128)S(1)}, u32[]{:S(2)}, u32[]{:S(2)}) collective-permute-start(f32[48,384]{1,0:T(8,128)S(1)} %add.338), channel_id=1, source_target_pairs={{0,64},{32,96},{64,128},{96,160},{128,192},{160,224},{192,0},{224,... | collective-permute-start | bytes 221192 | tf_op jit(solution)/shard_map/ppermute | solution.py:29
  109.8 2.9 %collective-permute-start.34 = (f32[48,384]{1,0:T(8,128)S(1)}, f32[48,384]{1,0:T(8,128)S(1)}, u32[]{:S(2)}, u32[]{:S(2)}) collective-permute-start(f32[48,384]{1,0:T(8,128)S(1)} %add.338), channel_id=1, source_target_pairs={{0,192},{32,224},{64,0},{96,32},{128,64},{160,96},{192,128},{224,1... | collective-permute-start | bytes 221192 | tf_op jit(solution)/shard_map/ppermute | solution.py:29
  113.1 1.1 collective-permute-start.24
  114.2 1.5 %collective-permute-start.25 = (f32[32,384]{1,0:T(8,128)S(1)}, f32[32,384]{1,0:T(8,128)S(1)}, u32[]{:S(2)}, u32[]{:S(2)}) collective-permute-start(f32[32,384]{1,0:T(8,128)S(1)} %get-tuple-element.31), channel_id=1, source_target_pairs={{0,64},{32,96},{64,128},{96,160},{128,192},{160,224},{192,0},{224,... | collective-permute-start | bytes 147464 | tf_op jit(solution)/shard_map/ppermute | solution.py:29
  115.7 2.6 %collective-permute-start.26 = (f32[32,384]{1,0:T(8,128)S(1)}, f32[32,384]{1,0:T(8,128)S(1)}, u32[]{:S(2)}, u32[]{:S(2)}) collective-permute-start(f32[32,384]{1,0:T(8,128)S(1)} %get-tuple-element.30), channel_id=1, source_target_pairs={{0,192},{32,224},{64,0},{96,32},{128,64},{160,96},{192,128},{224,1... | collective-permute-start | bytes 147464 | tf_op jit(solution)/shard_map/ppermute | solution.py:29
  118.3 3.3 %collective-permute-start.35 = (f32[48,384]{1,0:T(8,128)S(1)}, f32[48,384]{1,0:T(8,128)S(1)}, u32[]{:S(2)}, u32[]{:S(2)}) collective-permute-start(f32[48,384]{1,0:T(8,128)S(1)} %add_add_fusion), channel_id=1, source_target_pairs={{0,17},{8,25},{2,19},{10,27},{4,21},{12,29},{6,23},{14,31},{1,0},{... | collective-permute-start | bytes 221192 | tf_op jit(solution)/shard_map/ppermute | solution.py:21
  121.9 2.3 %collective-permute-start.36 = (f32[48,384]{1,0:T(8,128)S(1)}, f32[48,384]{1,0:T(8,128)S(1)}, u32[]{:S(2)}, u32[]{:S(2)}) collective-permute-start(f32[48,384]{1,0:T(8,128)S(1)} %add_add_fusion), channel_id=1, source_target_pairs={{0,16},{8,24},{2,18},{10,26},{4,20},{12,28},{6,22},{14,30},{1,17},... | collective-permute-start | bytes 221192 | tf_op jit(solution)/shard_map/ppermute | solution.py:21
  124.2 1.8 %collective-permute-start.37 = (f32[48,384]{1,0:T(8,128)S(1)}, f32[48,384]{1,0:T(8,128)S(1)}, u32[]{:S(2)}, u32[]{:S(2)}) collective-permute-start(f32[48,384]{1,0:T(8,128)S(1)} %add_add_fusion), channel_id=1, source_target_pairs={{0,1},{8,9},{2,3},{10,11},{4,5},{12,13},{6,7},{14,15},{1,16},{9,24... | collective-permute-start | bytes 221192 | tf_op jit(solution)/shard_map/ppermute | solution.py:21
  126.7 3.7 %collective-permute-start.28 = (f32[32,384]{1,0:T(8,128)S(1)}, f32[32,384]{1,0:T(8,128)S(1)}, u32[]{:S(2)}, u32[]{:S(2)}) collective-permute-start(f32[32,384]{1,0:T(8,128)S(1)} %add_add_fusion.2), channel_id=1, source_target_pairs={{0,128},{32,160},{64,192},{96,224},{128,0},{160,32},{192,64},{224,... | collective-permute-start | bytes 147464 | tf_op jit(solution)/shard_map/ppermute | solution.py:29
  130.8 0.8 collective-permute-done.27
  131.6 3.4 %collective-permute-done.28 = f32[32,384]{1,0:T(8,128)S(1)} collective-permute-done((f32[32,384]{1,0:T(8,128)S(1)}, f32[32,384]{1,0:T(8,128)S(1)}, u32[]{:S(2)}, u32[]{:S(2)}) %collective-permute-start.28) | collective-permute-done | bytes 49184 | tf_op jit(solution)/shard_map/ppermute | solution.py:29
  135.0 1.6 %collective-permute-done.29 = f32[32,384]{1,0:T(8,128)S(1)} collective-permute-done((f32[32,384]{1,0:T(8,128)S(1)}, f32[32,384]{1,0:T(8,128)S(1)}, u32[]{:S(2)}, u32[]{:S(2)}) %collective-permute-start.29) | collective-permute-done | bytes 49184 | tf_op jit(solution)/shard_map/ppermute | solution.py:29
  136.7 0.9 collective-permute-start.30
  137.8 1.1 fusion.4
  138.9 3.6 %collective-permute-done.30 = f32[128,384]{1,0:T(8,128)S(1)} collective-permute-done((f32[128,384]{1,0:T(8,128)S(1)}, f32[128,384]{1,0:T(8,128)S(1)}, u32[]{:S(2)}, u32[]{:S(2)}) %collective-permute-start.30) | collective-permute-done | bytes 196640 | tf_op jit(solution)/shard_map/ppermute | solution.py:33
  142.5 0.9 fusion.6
  143.4 1.1 fusion.1
  (97 shorter events, 8.1 us)
Async XLA Ops:
  0.6 18.8 %copy-start = (s32[32]{0:T(128)S(1)}, s32[32]{0:T(128)}, u32[]{:S(2)}) copy-start(s32[32]{0:T(128)} %param.9) | copy-start | bytes 388
  0.6 27.4 %copy-start.3 = (f32[1,256,384]{2,1,0:T(8,128)S(1)}, f32[1,256,384]{2,1,0:T(8,128)}, u32[]{:S(2)}) copy-start(f32[1,256,384]{2,1,0:T(8,128)} %param.6) | copy-start | bytes 1179652
  0.7 18.1 %collective-permute-start = (f32[256,384]{1,0:T(8,128)}, f32[256,384]{1,0:T(8,128)S(1)}, u32[]{:S(2)}, u32[]{:S(2)}) collective-permute-start(f32[256,384]{1,0:T(8,128)} %bitcast.38), channel_id=1, source_target_pairs={{0,0},{2,8},{8,2},{10,10},{16,4},{18,12},{24,6},{26,14},{4,1},{6,9... | collective-permute-start | bytes 1179656 | tf_op jit(solution)/shard_map/ppermute | solution.py:42
  2.7 16.1 %collective-permute-start.1 = (f32[256,384]{1,0:T(8,128)}, f32[256,384]{1,0:T(8,128)S(1)}, u32[]{:S(2)}, u32[]{:S(2)}) collective-permute-start(f32[256,384]{1,0:T(8,128)} %bitcast.39), channel_id=1, source_target_pairs={{1,0},{3,8},{9,2},{11,10},{17,4},{19,12},{25,6},{27,14},{5,1},{7,9... | collective-permute-start | bytes 1179656 | tf_op jit(solution)/shard_map/ppermute | solution.py:42
  18.8 1.7 %collective-permute-start.2 = (f32[256,384]{1,0:T(8,128)S(1)}, f32[256,384]{1,0:T(8,128)S(1)}, u32[]{:S(2)}, u32[]{:S(2)}) collective-permute-start(f32[256,384]{1,0:T(8,128)S(1)} %collective-permute-done.s0), channel_id=1, source_target_pairs={{0,8},{8,0},{2,10},{10,2},{4,12},{12,4},{6,14},{14,6},{1,9},{9,1},... | collective-permute-start | bytes 1179656 | tf_op jit(solution)/shard_map/ppermute | solution.py:21
  18.8 2.3 %collective-permute-start.3 = (f32[256,384]{1,0:T(8,128)S(1)}, f32[256,384]{1,0:T(8,128)S(1)}, u32[]{:S(2)}, u32[]{:S(2)}) collective-permute-start(f32[256,384]{1,0:T(8,128)S(1)} %collective-permute-done.1.s1), channel_id=1, source_target_pairs={{0,8},{8,0},{2,10},{10,2},{4,12},{12,4},{6,14},{14,6},{1,9},{9,1},... | collective-permute-start | bytes 1179656 | tf_op jit(solution)/shard_map/ppermute | solution.py:21
  21.1 3.4 %copy-start.1 = (f32[1,2048,1024]{2,1,0:T(8,128)S(1)}, f32[1,2048,1024]{2,1,0:T(8,128)}, u32[]{:S(2)}) copy-start(f32[1,2048,1024]{2,1,0:T(8,128)} %param.5) | copy-start | bytes 25165828
  27.4 18.4 %collective-permute-start.8 = (f32[256,384]{1,0:T(8,128)S(1)}, f32[256,384]{1,0:T(8,128)}, u32[]{:S(2)}, u32[]{:S(2)}) collective-permute-start(f32[256,384]{1,0:T(8,128)S(1)} %get-tuple-element.22), channel_id=1, source_target_pairs={{0,6},{8,14},{2,0},{10,8},{4,2},{12,10},{6,4},{14,12},{1,7},{9,15}... | collective-permute-start | bytes 1179656 | tf_op jit(solution)/shard_map/ppermute | solution.py:21
  28.0 26.8 %collective-permute-start.10 = (f32[256,384]{1,0:T(8,128)S(1)}, f32[256,384]{1,0:T(8,128)S(1)}, u32[]{:S(2)}, u32[]{:S(2)}) collective-permute-start(f32[256,384]{1,0:T(8,128)S(1)} %bitcast.40), channel_id=1, source_target_pairs={{0,1},{8,9},{2,3},{10,11},{4,5},{12,13},{6,7},{14,15},{1,0},{9,8},... | collective-permute-start | bytes 1179656 | tf_op jit(solution)/shard_map/ppermute | solution.py:25
  36.6 15.1 %collective-permute-start.4 = (f32[256,384]{1,0:T(8,128)S(1)}, f32[256,384]{1,0:T(8,128)S(1)}, u32[]{:S(2)}, u32[]{:S(2)}) collective-permute-start(f32[256,384]{1,0:T(8,128)S(1)} %get-tuple-element.23), channel_id=1, source_target_pairs={{0,2},{8,10},{2,4},{10,12},{4,6},{12,14},{6,0},{14,8},{1,3},{9,11}... | collective-permute-start | bytes 1179656 | tf_op jit(solution)/shard_map/ppermute | solution.py:21
  37.2 3.4 %copy-start.2 = (f32[1,2048,1024]{2,1,0:T(8,128)S(1)}, f32[1,2048,1024]{2,1,0:T(8,128)}, u32[]{:S(2)}) copy-start(f32[1,2048,1024]{2,1,0:T(8,128)} %param.5) | copy-start | bytes 25165828
  46.9 12.1 %collective-permute-start.7 = (f32[256,384]{1,0:T(8,128)S(1)}, f32[256,384]{1,0:T(8,128)S(1)}, u32[]{:S(2)}, u32[]{:S(2)}) collective-permute-start(f32[256,384]{1,0:T(8,128)S(1)} %get-tuple-element.21), channel_id=1, source_target_pairs={{0,6},{8,14},{2,0},{10,8},{4,2},{12,10},{6,4},{14,12},{1,7},{9,15}... | collective-permute-start | bytes 1179656 | tf_op jit(solution)/shard_map/ppermute | solution.py:21
  48.5 17.8 %collective-permute-start.9 = (f32[256,384]{1,0:T(8,128)S(1)}, f32[256,384]{1,0:T(8,128)S(1)}, u32[]{:S(2)}, u32[]{:S(2)}) collective-permute-start(f32[256,384]{1,0:T(8,128)S(1)} %get-tuple-element.20), channel_id=1, source_target_pairs={{0,6},{8,14},{2,0},{10,8},{4,2},{12,10},{6,4},{14,12},{1,7},{9,15}... | collective-permute-start | bytes 1179656 | tf_op jit(solution)/shard_map/ppermute | solution.py:21
  51.8 14.5 %collective-permute-start.5 = (f32[256,384]{1,0:T(8,128)S(1)}, f32[256,384]{1,0:T(8,128)S(1)}, u32[]{:S(2)}, u32[]{:S(2)}) collective-permute-start(f32[256,384]{1,0:T(8,128)S(1)} %get-tuple-element.25), channel_id=1, source_target_pairs={{0,2},{8,10},{2,4},{10,12},{4,6},{12,14},{6,0},{14,8},{1,3},{9,11}... | collective-permute-start | bytes 1179656 | tf_op jit(solution)/shard_map/ppermute | solution.py:21
  51.8 18.5 %collective-permute-start.6 = (f32[256,384]{1,0:T(8,128)S(1)}, f32[256,384]{1,0:T(8,128)S(1)}, u32[]{:S(2)}, u32[]{:S(2)}) collective-permute-start(f32[256,384]{1,0:T(8,128)S(1)} %get-tuple-element.24), channel_id=1, source_target_pairs={{0,2},{8,10},{2,4},{10,12},{4,6},{12,14},{6,0},{14,8},{1,3},{9,11}... | collective-permute-start | bytes 1179656 | tf_op jit(solution)/shard_map/ppermute | solution.py:21
  71.8 2.0 %collective-permute-start.12 = (f32[192,384]{1,0:T(8,128)S(1)}, f32[192,384]{1,0:T(8,128)S(1)}, u32[]{:S(2)}, u32[]{:S(2)}) collective-permute-start(f32[192,384]{1,0:T(8,128)S(1)} %constant_dynamic-slice_fusion.10), channel_id=1, source_target_pairs={{0,8},{8,0},{2,10},{10,2},{4,12},{12,4},{6,14},{14,6},{1,9},{9,1},... | collective-permute-start | bytes 884744 | tf_op jit(solution)/shard_map/ppermute | solution.py:21
  72.0 17.8 %collective-permute-start.11 = (f32[256,384]{1,0:T(8,128)S(1)}, f32[256,384]{1,0:T(8,128)S(1)}, u32[]{:S(2)}, u32[]{:S(2)}) collective-permute-start(f32[256,384]{1,0:T(8,128)S(1)} %get-tuple-element.14), channel_id=1, source_target_pairs={{0,1},{8,9},{2,3},{10,11},{4,5},{12,13},{6,7},{14,15},{1,0},{9,8},... | collective-permute-start | bytes 1179656 | tf_op jit(solution)/shard_map/ppermute | solution.py:25
  73.9 11.9 %collective-permute-start.13 = (f32[48,384]{1,0:T(8,128)S(1)}, f32[48,384]{1,0:T(8,128)S(1)}, u32[]{:S(2)}, u32[]{:S(2)}) collective-permute-start(f32[48,384]{1,0:T(8,128)S(1)} %get-tuple-element.26), channel_id=1, source_target_pairs={{0,16},{8,24},{2,18},{10,26},{4,20},{12,28},{6,22},{14,30},{1,17},... | collective-permute-start | bytes 221192 | tf_op jit(solution)/shard_map/ppermute | solution.py:21
  75.5 10.3 %collective-permute-start.14 = (f32[48,384]{1,0:T(8,128)S(1)}, f32[48,384]{1,0:T(8,128)S(1)}, u32[]{:S(2)}, u32[]{:S(2)}) collective-permute-start(f32[48,384]{1,0:T(8,128)S(1)} %get-tuple-element.28), channel_id=1, source_target_pairs={{0,1},{8,9},{2,3},{10,11},{4,5},{12,13},{6,7},{14,15},{1,16},{9,24... | collective-permute-start | bytes 221192 | tf_op jit(solution)/shard_map/ppermute | solution.py:21
  75.6 11.1 %collective-permute-start.15 = (f32[48,384]{1,0:T(8,128)S(1)}, f32[48,384]{1,0:T(8,128)S(1)}, u32[]{:S(2)}, u32[]{:S(2)}) collective-permute-start(f32[48,384]{1,0:T(8,128)S(1)} %get-tuple-element.27), channel_id=1, source_target_pairs={{0,17},{8,25},{2,19},{10,27},{4,21},{12,29},{6,23},{14,31},{1,0},{... | collective-permute-start | bytes 221192 | tf_op jit(solution)/shard_map/ppermute | solution.py:21
  86.6 6.7 %collective-permute-start.16 = (f32[48,384]{1,0:T(8,128)S(1)}, f32[48,384]{1,0:T(8,128)S(1)}, u32[]{:S(2)}, u32[]{:S(2)}) collective-permute-start(f32[48,384]{1,0:T(8,128)S(1)} %add_add_fusion.1), channel_id=1, source_target_pairs={{0,4},{8,12},{2,6},{10,14},{4,0},{12,8},{6,2},{14,10},{1,5},{9,13}... | collective-permute-start | bytes 221192 | tf_op jit(solution)/shard_map/ppermute | solution.py:21
  87.2 6.2 %collective-permute-start.17 = (f32[48,384]{1,0:T(8,128)S(1)}, f32[48,384]{1,0:T(8,128)S(1)}, u32[]{:S(2)}, u32[]{:S(2)}) collective-permute-start(f32[48,384]{1,0:T(8,128)S(1)} %add_add_fusion.1), channel_id=1, source_target_pairs={{0,2},{8,10},{2,4},{10,12},{4,6},{12,14},{6,0},{14,8},{1,3},{9,11}... | collective-permute-start | bytes 221192 | tf_op jit(solution)/shard_map/ppermute | solution.py:21
  89.8 4.4 %collective-permute-start.18 = (f32[48,384]{1,0:T(8,128)S(1)}, f32[48,384]{1,0:T(8,128)S(1)}, u32[]{:S(2)}, u32[]{:S(2)}) collective-permute-start(f32[48,384]{1,0:T(8,128)S(1)} %add_add_fusion.1), channel_id=1, source_target_pairs={{0,6},{8,14},{2,0},{10,8},{4,2},{12,10},{6,4},{14,12},{1,7},{9,15}... | collective-permute-start | bytes 221192 | tf_op jit(solution)/shard_map/ppermute | solution.py:21
  95.0 6.0 %collective-permute-start.31 = (f32[48,384]{1,0:T(8,128)S(1)}, f32[48,384]{1,0:T(8,128)S(1)}, u32[]{:S(2)}, u32[]{:S(2)}) collective-permute-start(f32[48,384]{1,0:T(8,128)S(1)} %get-tuple-element.16), channel_id=1, source_target_pairs={{0,32},{32,0},{64,96},{96,64},{128,160},{160,128},{192,224},{224,1... | collective-permute-start | bytes 221192 | tf_op jit(solution)/shard_map/ppermute | solution.py:33
  97.0 11.3 %collective-permute-start.19 = (f32[48,384]{1,0:T(8,128)S(1)}, f32[48,384]{1,0:T(8,128)S(1)}, u32[]{:S(2)}, u32[]{:S(2)}) collective-permute-start(f32[48,384]{1,0:T(8,128)S(1)} %get-tuple-element.17), channel_id=1, source_target_pairs={{0,17},{8,25},{2,19},{10,27},{4,21},{12,29},{6,23},{14,31},{1,0},{... | collective-permute-start | bytes 221192 | tf_op jit(solution)/shard_map/ppermute | solution.py:21
  98.7 14.3 %collective-permute-start.23 = (f32[128,384]{1,0:T(8,128)S(1)}, f32[128,384]{1,0:T(8,128)S(1)}, u32[]{:S(2)}, u32[]{:S(2)}) collective-permute-start(f32[128,384]{1,0:T(8,128)S(1)} %constant_dynamic-slice_fusion.5), channel_id=1, source_target_pairs={{0,32},{32,0},{64,96},{96,64},{128,160},{160,128},{192,224},{224,1... | collective-permute-start | bytes 589832 | tf_op jit(solution)/shard_map/ppermute | solution.py:33
  98.9 10.9 %collective-permute-start.20 = (f32[48,384]{1,0:T(8,128)S(1)}, f32[48,384]{1,0:T(8,128)S(1)}, u32[]{:S(2)}, u32[]{:S(2)}) collective-permute-start(f32[48,384]{1,0:T(8,128)S(1)} %get-tuple-element.17), channel_id=1, source_target_pairs={{0,16},{8,24},{2,18},{10,26},{4,20},{12,28},{6,22},{14,30},{1,17},... | collective-permute-start | bytes 221192 | tf_op jit(solution)/shard_map/ppermute | solution.py:21
  101.1 11.7 %collective-permute-start.21 = (f32[48,384]{1,0:T(8,128)S(1)}, f32[48,384]{1,0:T(8,128)S(1)}, u32[]{:S(2)}, u32[]{:S(2)}) collective-permute-start(f32[48,384]{1,0:T(8,128)S(1)} %get-tuple-element.17), channel_id=1, source_target_pairs={{0,1},{8,9},{2,3},{10,11},{4,5},{12,13},{6,7},{14,15},{1,16},{9,24... | collective-permute-start | bytes 221192 | tf_op jit(solution)/shard_map/ppermute | solution.py:21
  101.1 13.1 %collective-permute-start.32 = (f32[48,384]{1,0:T(8,128)S(1)}, f32[48,384]{1,0:T(8,128)S(1)}, u32[]{:S(2)}, u32[]{:S(2)}) collective-permute-start(f32[48,384]{1,0:T(8,128)S(1)} %add.338), channel_id=1, source_target_pairs={{0,128},{32,160},{64,192},{96,224},{128,0},{160,32},{192,64},{224,... | collective-permute-start | bytes 221192 | tf_op jit(solution)/shard_map/ppermute | solution.py:29
  108.3 7.3 %collective-permute-start.33 = (f32[48,384]{1,0:T(8,128)S(1)}, f32[48,384]{1,0:T(8,128)S(1)}, u32[]{:S(2)}, u32[]{:S(2)}) collective-permute-start(f32[48,384]{1,0:T(8,128)S(1)} %add.338), channel_id=1, source_target_pairs={{0,64},{32,96},{64,128},{96,160},{128,192},{160,224},{192,0},{224,... | collective-permute-start | bytes 221192 | tf_op jit(solution)/shard_map/ppermute | solution.py:29
  109.8 8.4 %collective-permute-start.34 = (f32[48,384]{1,0:T(8,128)S(1)}, f32[48,384]{1,0:T(8,128)S(1)}, u32[]{:S(2)}, u32[]{:S(2)}) collective-permute-start(f32[48,384]{1,0:T(8,128)S(1)} %add.338), channel_id=1, source_target_pairs={{0,192},{32,224},{64,0},{96,32},{128,64},{160,96},{192,128},{224,1... | collective-permute-start | bytes 221192 | tf_op jit(solution)/shard_map/ppermute | solution.py:29
  112.9 24.9 %collective-permute-start.22 = (f32[192,384]{1,0:T(8,128)S(1)}, f32[192,384]{1,0:T(8,128)S(1)}, u32[]{:S(2)}, u32[]{:S(2)}) collective-permute-start(f32[192,384]{1,0:T(8,128)S(1)} %constant_dynamic-slice_fusion.6), channel_id=1, source_target_pairs={{0,8},{8,0},{2,10},{10,2},{4,12},{12,4},{6,14},{14,6},{1,9},{9,1},... | collective-permute-start | bytes 884744 | tf_op jit(solution)/shard_map/ppermute | solution.py:21
  113.1 8.8 %collective-permute-start.24 = (f32[32,384]{1,0:T(8,128)S(1)}, f32[32,384]{1,0:T(8,128)S(1)}, u32[]{:S(2)}, u32[]{:S(2)}) collective-permute-start(f32[32,384]{1,0:T(8,128)S(1)} %get-tuple-element.29), channel_id=1, source_target_pairs={{0,128},{32,160},{64,192},{96,224},{128,0},{160,32},{192,64},{224,... | collective-permute-start | bytes 147464 | tf_op jit(solution)/shard_map/ppermute | solution.py:29
  114.2 10.0 %collective-permute-start.25 = (f32[32,384]{1,0:T(8,128)S(1)}, f32[32,384]{1,0:T(8,128)S(1)}, u32[]{:S(2)}, u32[]{:S(2)}) collective-permute-start(f32[32,384]{1,0:T(8,128)S(1)} %get-tuple-element.31), channel_id=1, source_target_pairs={{0,64},{32,96},{64,128},{96,160},{128,192},{160,224},{192,0},{224,... | collective-permute-start | bytes 147464 | tf_op jit(solution)/shard_map/ppermute | solution.py:29
  115.7 10.3 %collective-permute-start.26 = (f32[32,384]{1,0:T(8,128)S(1)}, f32[32,384]{1,0:T(8,128)S(1)}, u32[]{:S(2)}, u32[]{:S(2)}) collective-permute-start(f32[32,384]{1,0:T(8,128)S(1)} %get-tuple-element.30), channel_id=1, source_target_pairs={{0,192},{32,224},{64,0},{96,32},{128,64},{160,96},{192,128},{224,1... | collective-permute-start | bytes 147464 | tf_op jit(solution)/shard_map/ppermute | solution.py:29
  118.3 8.4 %collective-permute-start.35 = (f32[48,384]{1,0:T(8,128)S(1)}, f32[48,384]{1,0:T(8,128)S(1)}, u32[]{:S(2)}, u32[]{:S(2)}) collective-permute-start(f32[48,384]{1,0:T(8,128)S(1)} %add_add_fusion), channel_id=1, source_target_pairs={{0,17},{8,25},{2,19},{10,27},{4,21},{12,29},{6,23},{14,31},{1,0},{... | collective-permute-start | bytes 221192 | tf_op jit(solution)/shard_map/ppermute | solution.py:21
  121.9 8.5 %collective-permute-start.36 = (f32[48,384]{1,0:T(8,128)S(1)}, f32[48,384]{1,0:T(8,128)S(1)}, u32[]{:S(2)}, u32[]{:S(2)}) collective-permute-start(f32[48,384]{1,0:T(8,128)S(1)} %add_add_fusion), channel_id=1, source_target_pairs={{0,16},{8,24},{2,18},{10,26},{4,20},{12,28},{6,22},{14,30},{1,17},... | collective-permute-start | bytes 221192 | tf_op jit(solution)/shard_map/ppermute | solution.py:21
  124.2 6.6 %collective-permute-start.37 = (f32[48,384]{1,0:T(8,128)S(1)}, f32[48,384]{1,0:T(8,128)S(1)}, u32[]{:S(2)}, u32[]{:S(2)}) collective-permute-start(f32[48,384]{1,0:T(8,128)S(1)} %add_add_fusion), channel_id=1, source_target_pairs={{0,1},{8,9},{2,3},{10,11},{4,5},{12,13},{6,7},{14,15},{1,16},{9,24... | collective-permute-start | bytes 221192 | tf_op jit(solution)/shard_map/ppermute | solution.py:21
  126.0 5.6 %collective-permute-start.27 = (f32[32,384]{1,0:T(8,128)S(1)}, f32[32,384]{1,0:T(8,128)S(1)}, u32[]{:S(2)}, u32[]{:S(2)}) collective-permute-start(f32[32,384]{1,0:T(8,128)S(1)} %add_add_fusion.2), channel_id=1, source_target_pairs={{0,192},{32,224},{64,0},{96,32},{128,64},{160,96},{192,128},{224,1... | collective-permute-start | bytes 147464 | tf_op jit(solution)/shard_map/ppermute | solution.py:29
  126.7 8.4 %collective-permute-start.28 = (f32[32,384]{1,0:T(8,128)S(1)}, f32[32,384]{1,0:T(8,128)S(1)}, u32[]{:S(2)}, u32[]{:S(2)}) collective-permute-start(f32[32,384]{1,0:T(8,128)S(1)} %add_add_fusion.2), channel_id=1, source_target_pairs={{0,128},{32,160},{64,192},{96,224},{128,0},{160,32},{192,64},{224,... | collective-permute-start | bytes 147464 | tf_op jit(solution)/shard_map/ppermute | solution.py:29
  130.4 6.3 %collective-permute-start.29 = (f32[32,384]{1,0:T(8,128)S(1)}, f32[32,384]{1,0:T(8,128)S(1)}, u32[]{:S(2)}, u32[]{:S(2)}) collective-permute-start(f32[32,384]{1,0:T(8,128)S(1)} %add_add_fusion.2), channel_id=1, source_target_pairs={{0,64},{32,96},{64,128},{96,160},{128,192},{160,224},{192,0},{224,... | collective-permute-start | bytes 147464 | tf_op jit(solution)/shard_map/ppermute | solution.py:29
  136.7 5.8 %collective-permute-start.30 = (f32[128,384]{1,0:T(8,128)S(1)}, f32[128,384]{1,0:T(8,128)S(1)}, u32[]{:S(2)}, u32[]{:S(2)}) collective-permute-start(f32[128,384]{1,0:T(8,128)S(1)} %constant_dynamic-slice_fusion.1), channel_id=1, source_target_pairs={{0,32},{32,0},{64,96},{96,64},{128,160},{160,128},{192,224},{224,1... | collective-permute-start | bytes 589832 | tf_op jit(solution)/shard_map/ppermute | solution.py:33
  137.7 5.7 %collective-permute-start.38 = (f32[192,384]{1,0:T(8,128)S(1)}, f32[192,384]{1,0:T(8,128)S(1)}, u32[]{:S(2)}, u32[]{:S(2)}) collective-permute-start(f32[192,384]{1,0:T(8,128)S(1)} %constant_dynamic-slice_fusion), channel_id=1, source_target_pairs={{0,8},{8,0},{2,10},{10,2},{4,12},{12,4},{6,14},{14,6},{1,9},{9,1},... | collective-permute-start | bytes 884744 | tf_op jit(solution)/shard_map/ppermute | solution.py:21
